TPU v7x, 512 devices: a whole 4x4x16 slice. The times are simulated.
512 devices in a mesh: dp: 8 (over z_hi, y), vocab: 64 (over z_lo, x, core).
Axes of the slice: x: 4, y: 4, z: 16 (z_hi: 2, z_lo: 8; z = z_hi * 8 + z_lo), core: 2. Of those that a mesh axis runs over, the one named last changes fastest.
Arguments:
- hidden: bfloat16 [1024, 5120], P('dp', 'vocab'), may hold values from -8 to 8
- head_weight: bfloat16 [5120, 76032], P('dp', 'vocab'), may hold values from -0.25 to 0.25
- teacher_logits: bfloat16 [1024, 76032], P(('dp', 'vocab')), may hold values from -30 to 330
- block_owner: int32 [64], replicated, may hold values from 0 to 63, each once
- sampled_ids: int32 [1024], P('dp'), may hold values from 0 to 76031
- loss_weight: float32 [1024], P('dp'), may hold values from 1 to 10
Outputs:
- grad_hidden: float32 [1024, 5120], P('dp', 'vocab')
- divergence: float32 [1024], P('dp')
- sampled_logp: float32 [1024], P('dp')
Inputs may be any that keep to these rules, and one draw needn't show every extreme that they name: `block_owner`: each of the 64 numbers appears once.
All inputs are finite; a program needn't handle non-finite values.
Results may differ from a plain program's by a relative error of at most 0.003.
Values may be sent and summed in bfloat16 or wider, within the bound.
A program may use at most 64 MiB of HBM per device.

v0:
```python
import jax
import jax.numpy as jnp
from jax import lax
from jax.sharding import PartitionSpec as P


def on_device(hidden, head_weight, teacher_logits, block_owner, sampled_ids, loss_weight):
    block_count = lax.axis_size("vocab")
    vocab_index = lax.axis_index("vocab")
    tok_rows = teacher_logits.shape[0]
    full_width = teacher_logits.shape[1]
    vocab_dev = head_weight.shape[1]
    teacher_blocks = teacher_logits.reshape(tok_rows, block_count, vocab_dev)
    reordered = jnp.zeros_like(teacher_blocks).at[:, block_owner].set(teacher_blocks)
    reordered = reordered.reshape(tok_rows, full_width)
    received = lax.all_to_all(reordered, "vocab", split_axis=1, concat_axis=0, tiled=True)
    features = lax.all_gather(hidden, "vocab", axis=1, tiled=True)
    weights = lax.all_gather(head_weight, "dp", axis=0, tiled=True)
    logits = jnp.dot(features, weights, preferred_element_type=jnp.float32)
    teacher = received.astype(jnp.float32)
    gap_logits = logits - teacher
    columns = vocab_index * vocab_dev + lax.broadcasted_iota(jnp.int32, (1, vocab_dev), 1)
    picked_here = jnp.sum(jnp.where(columns == sampled_ids[:, None], logits, 0.0), axis=1)
    local_top = jnp.max(logits, axis=1)
    teacher_here = jnp.max(teacher, axis=1)
    student_top, teacher_top = lax.pmax((local_top, teacher_here), "vocab")
    student_exp = jnp.exp(logits - student_top[:, None])
    teacher_exp = jnp.exp(teacher - teacher_top[:, None])
    student_sum, weighted, picked, teacher_sum = lax.psum(
        (
            jnp.sum(student_exp, axis=1),
            jnp.sum(student_exp * gap_logits, axis=1),
            picked_here,
            jnp.sum(teacher_exp, axis=1),
        ),
        "vocab",
    )
    teacher_lse = teacher_top + jnp.log(teacher_sum)
    student_lse = student_top + jnp.log(student_sum)
    divergence = weighted / student_sum - student_lse + teacher_lse
    sampled_logp = picked - student_lse
    student_prob = jnp.exp(logits - student_lse[:, None])
    grad_logits = (
        loss_weight[:, None]
        * student_prob
        * (gap_logits - student_lse[:, None] + teacher_lse[:, None] - divergence[:, None])
    ).astype(jnp.bfloat16)
    partial_grad = lax.dot_general(
        grad_logits, weights, (((1,), (1,)), ((), ())), preferred_element_type=jnp.float32
    )
    grad_hidden = lax.psum_scatter(partial_grad, "vocab", scatter_dimension=1, tiled=True)
    return (grad_hidden, divergence, sampled_logp)


def solution(mesh):
    return jax.shard_map(
        on_device,
        mesh=mesh,
        in_specs=(
            P("dp", "vocab"),
            P("dp", "vocab"),
            P(("dp", "vocab"), None),
            P(),
            P("dp"),
            P("dp"),
        ),
        out_specs=(P("dp", "vocab"), P("dp"), P("dp")),
        check_vma=False,
    )
```

profile of v0, /device:TPU:16, one launch (start us, length us, event | category | flops | bytes accessed | tf_op | source)
XLA Modules:
  0.0 1417.6 jit_solution(12734442252915766227)
XLA Ops:
  7.2 0.7 all-gather.3.cloned.1.call-update
  8.0 0.7 all-gather.5.cloned.1.call-update
  8.7 1.9 reshape.41
  10.6 0.3 copy.14
  10.9 0.7 compare_select_fusion
  11.6 0.9 broadcast_in_dim.8
  12.5 8.0 scatter_fusion
  20.4 16.0 %all-to-all-start = ((bf16[2,64,1188]{2,0,1:T(2,128)(2,1)}), bf16[2,64,1188]{2,0,1:T(2,128)(2,1)S(1)}, u32[]{:S(2)}, u32[]{:S(2)}) async-start(bf16[2,64,1188]{2,0,1:T(2,128)(2,1)} %scatter_fusion), calls=%async_computation | async-start | bytes 655360 | tf_op jit(solution)/shard_map/all_to_all | solution.py:16
  36.5 23.2 %all-to-all-done = bf16[2,64,1188]{2,0,1:T(2,128)(2,1)S(1)} async-done(((bf16[2,64,1188]{2,0,1:T(2,128)(2,1)}), bf16[2,64,1188]{2,0,1:T(2,128)(2,1)S(1)}, u32[]{:S(2)}, u32[]{:S(2)}) %all-to-all-start) | async-done | bytes 304160 | tf_op jit(solution)/shard_map/all_to_all | solution.py:16
  59.7 0.3 bitcast_reduce_fusion
  60.1 0.1 reshape.39
  60.2 0.2 bitcast_convert_fusion
  60.4 0.5 reshape.38
  60.9 0.2 copy.12
  61.1 75.8 %all-gather.3.cloned.1.call-done = bf16[128,5120]{0,1:T(8,128)(2,1)} async-done(((bf16[128,80]{0,1:T(8,128)(2,1)}), bf16[128,5120]{0,1:T(8,128)(2,1)}) %all-gather.3.cloned.1.call-update) | async-done | bytes 1310736 | tf_op jit(solution)/shard_map/all_gather | solution.py:17
  137.0 397.9 %all-gather.5.cloned.1.call-done = bf16[5120,1188]{0,1:T(8,128)(2,1)} async-done(((bf16[640,1188]{0,1:T(8,128)(2,1)}), bf16[5120,1188]{0,1:T(8,128)(2,1)}) %all-gather.5.cloned.1.call-update) | async-done | bytes 12165136 | tf_op jit(solution)/shard_map/all_gather | solution.py:18
  534.8 6.7 fusion.8
  541.6 211.0 %all-reduce.1 = (f32[128]{0:T(128)S(1)}, f32[128]{0:T(128)S(1)}) all-reduce(f32[128]{0:T(128)S(1)} %reshape.39, f32[128]{0:T(128)S(1)} %get-tuple-element.16), channel_id=1, replica_groups=mesh['dp'=8,'vocab'=64] {'vocab'}, use_global_device_ids=true, to_apply=%region_6.7 | all-reduce | flops 256 | bytes 2048 | tf_op jit(solution)/shard_map/pmax | solution.py:26
  752.7 0.7 exponential_reduce_fusion
  753.5 0.3 multiply_reduce_fusion
  753.8 210.5 %all-reduce = (f32[128]{0:T(128)S(1)}, f32[128]{0:T(128)S(1)}, f32[128]{0:T(128)S(1)}, f32[128]{0:T(128)S(1)}) all-reduce(f32[128]{0:T(128)S(1)} %reduce_sum.40, f32[128]{0:T(128)S(1)} %get-tuple-element.4, f32[128]{0:T(128)S(1)} %get-tuple-element.3, f32[128]{0:T(128)S(1)} %get-tuple-element.5), channel_id=1, replica_groups=mesh['dp'=8,'vocab'=64] {'vocab'}, use_global_device_ids=true, to_apply=%region_8.9 | all-reduce | flops 512 | bytes 4096 | tf_op jit(solution)/shard_map/psum | solution.py:29
  964.3 0.5 fusion.7
  964.9 11.2 fusion.1
  976.1 435.0 %reduce-scatter.2.cloned.1.call-done = f32[128,80]{0,1:T(8,128)} async-done(((f32[128,5120]{0,1:T(8,128)}), f32[128,80]{0,1:T(8,128)}) %reduce-scatter.2.cloned.1.call-update) | async-done | bytes 40976 | tf_op jit(solution)/shard_map/reduce_scatter | solution.py:51
  (14 shorter events, 0.4 us)
Async XLA Ops:
  7.2 746.4 %copy-start.2 = (s32[128]{0:T(128)S(1)}, s32[128]{0:T(128)}, u32[]{:S(2)}) copy-start(s32[128]{0:T(128)} %param.10) | copy-start | bytes 1540
  7.2 129.8 %all-gather.3.cloned.1.call-start = ((), (), s32[]{:S(2)}) async-start(), calls=%async_computation.2 | async-start | bytes 1331200 | tf_op jit(solution)/shard_map/all_gather | solution.py:17
  7.9 957.0 %copy-start.1 = (f32[128]{0:T(128)S(1)}, f32[128]{0:T(128)}, u32[]{:S(2)}) copy-start(f32[128]{0:T(128)} %param.11) | copy-start | bytes 1540
  7.9 526.9 %all-gather.5.cloned.1.call-start = ((), (), s32[]{:S(2)}) async-start(), calls=%async_computation.3 | async-start | bytes 13731840 | tf_op jit(solution)/shard_map/all_gather | solution.py:18
  20.4 39.3 %all-to-all-start = ((bf16[2,64,1188]{2,0,1:T(2,128)(2,1)}), bf16[2,64,1188]{2,0,1:T(2,128)(2,1)S(1)}, u32[]{:S(2)}, u32[]{:S(2)}) async-start(bf16[2,64,1188]{2,0,1:T(2,128)(2,1)} %scatter_fusion), calls=%async_computation | async-start | bytes 655360 | tf_op jit(solution)/shard_map/all_to_all | solution.py:16
  36.4 1374.6 %reduce-scatter.2.cloned.1.call-start = ((), (), s32[]{:S(2)}) async-start(), calls=%async_computation.4 | async-start | bytes 2662400 | tf_op jit(solution)/shard_map/reduce_scatter | solution.py:51
  964.9 446.2 %copy-start = (f32[128]{0:T(128)}, f32[128]{0:T(128)S(1)}, u32[]{:S(2)}) copy-start(f32[128]{0:T(128)S(1)} %get-tuple-element.14) | copy-start | bytes 1540
Sparse Core Ops, SparseCore 0:
  10.2 126.7 all-gather.2
  140.2 394.6 all-gather.4
  976.2 434.7 reduce-scatter.1
where the time goes:
time: 1420 us
  waiting for transfers between devices  933 us (66%)
  blocking collectives  422 us (30%)
  matrix products  17.9 us (1%)
  starting transfers between devices  16.1 us (1%)
    reduce_scatter x1, waiting for transfers between devices, on_device(): lax.psum_scatter(partial_grad, 'vocab', scatter_dimension=1, tiled=True)  435 us
    all_gather x1, waiting for transfers between devices, on_device(): weights = lax.all_gather(head_weight, 'dp', axis=0, tiled=True)  398 us
    pmax x1, blocking collectives, on_device(): student_top, teacher_top = lax.pmax((local_top, teacher_here), 'vocab')  211 us
    psum x1, blocking collectives, on_device(): lax.psum((jnp.sum(student_exp, axis=1), jnp.sum(student_exp * gap_logits,...  211 us
    all_gather x1, waiting for transfers between devices, on_device(): features = lax.all_gather(hidden, 'vocab', axis=1, tiled=True)  75.8 us
  transfers between devices with their start and end apart: 4, of which 4 were waited for; matrix products, arithmetic and copies ran while one was open for 1% of the time, Pallas kernels for 0%

commit v1 on v0

v1 whole, which is shorter than its diff:
```python
import jax
import jax.numpy as jnp
from jax import lax
from jax.experimental import pallas as pl
from jax.experimental.pallas import tpu as pltpu
from jax.sharding import PartitionSpec as P

MESH = pl.DeviceIdType.MESH
F32 = jnp.float32
BF16 = jnp.bfloat16

VD = 1188
VC = 256
NC = 5
VP = VC * NC
KS = 640
KH = 4 * KS
TK = 128
OB = 80


def kernel(
    inv_ref, hid_ref, w_ref, tea_ref, ids_ref, lw_ref,
    out_ref, tok_ref,
    Hb, hh, Wc, Sb, Rb, L, Fp, TP, TQ, F2, TR, TT,
    St, StA, St2, StB, Zt, GL, GT, RC, X1, RX, X2, RZ,
    s1s, s1r, s2s, s2r, s3s, s3r, ws, wr, zs_, zr_,
    tas, tar, tbs, tbr, sas, sar, sbs, sbr, gs, gr, cs, cr, xs, xr, rzs, rzr,
):
    dp = lax.axis_index("dp")
    v = lax.axis_index("vocab")
    h = lax.div(dp, 4)
    q = lax.rem(dp, 4)
    zl = lax.div(v, 8)
    e = lax.rem(v, 8)
    x = lax.div(e, 2)
    c = lax.rem(e, 2)
    z = h * 8 + zl
    oh = 1 - h
    hb = lax.div(zl, 4)
    ip = lax.rem(zl, 4)

    def at_z(zz):
        return (lax.div(zz, 8) * 4 + q, lax.rem(zz, 8) * 8 + e)

    def at_y(yy):
        return (h * 4 + yy, v)

    def at_e(ee):
        return (dp, zl * 8 + ee)

    partner = at_z(oh * 8 + zl)
    sibling = at_e(x * 2 + 1 - c)

    def copy(src, dst, ss, rs, dev):
        return pltpu.make_async_remote_copy(
            src_ref=src, dst_ref=dst, send_sem=ss, recv_sem=rs, device_id=dev, device_id_type=MESH
        )

    barrier = pltpu.get_barrier_semaphore()

    def greet_z(k, _):
        pl.semaphore_signal(barrier, inc=1, device_id=at_z(lax.rem(z + k, 16)), device_id_type=MESH)
        return _

    def greet_y(k, _):
        pl.semaphore_signal(barrier, inc=1, device_id=at_y(lax.rem(q + k, 4)), device_id_type=MESH)
        return _

    def greet_e(k, _):
        pl.semaphore_signal(barrier, inc=1, device_id=at_e(lax.rem(e + k, 8)), device_id_type=MESH)
        return _

    lax.fori_loop(1, 16, greet_z, 0)
    lax.fori_loop(1, 4, greet_y, 0)
    lax.fori_loop(1, 8, greet_e, 0)

    wrow = pl.multiple_of(q * KS, KS)
    for k in range(NC - 1):
        Wc[k, pl.ds(wrow, KS), :] = w_ref[:, k * VC:(k + 1) * VC]
    tail = VD - (NC - 1) * VC
    Wc[NC - 1, pl.ds(wrow, KS), :] = jnp.zeros((KS, VC), BF16)
    Wc[NC - 1, pl.ds(wrow, KS), 0:tail] = w_ref[:, (NC - 1) * VC:VD]

    pl.semaphore_wait(barrier, 25)

    def feat_copy(k):
        return copy(hid_ref, Hb.at[h, ip, x, c], s1s.at[k], s1r.at[h * 4 + ip], at_z(hb * 8 + k))

    def s1_send(k, _):
        @pl.when(hb * 8 + k != z)
        def _go():
            feat_copy(k).start()
        return _

    lax.fori_loop(0, 8, s1_send, 0)

    @pl.when(hb == h)
    def _own():
        Hb[h, ip, x, c] = hid_ref[...]

    def w_copy(ch, k):
        sl = Wc.at[ch, pl.ds(wrow, KS)]
        return copy(sl, sl, ws.at[ch * 3 + k - 1], wr.at[ch * 3 + k - 1], at_y(lax.rem(q + k, 4)))

    def w_send(ch):
        for k in (1, 3, 2):
            w_copy(ch, k).start()

    def w_wait_recv(ch):
        for k in (1, 2, 3):
            sl = Wc.at[ch, pl.ds(pl.multiple_of(lax.rem(q + 4 - k, 4) * KS, KS), KS)]
            copy(sl, sl, ws.at[ch * 3 + k - 1], wr.at[ch * 3 + k - 1], at_y(lax.rem(q + k, 4))).wait_recv()

    w_send(0)
    w_send(1)

    def pack(zz, _):
        for d in range(8):
            Fp[2 * d:2 * d + 2, :] = tea_ref[inv_ref[zz * 8 + d]]
        TP[zz] = Fp[...].astype(BF16)
        return _

    lax.fori_loop(0, 8, pack, 0)

    def ta_copy(k):
        to = lax.rem(zl + k, 8)
        return copy(TP.at[to], TQ.at[zl], tas.at[k - 1], tar.at[k - 1], at_z(h * 8 + to))

    def ta_send(k, _):
        ta_copy(k).start()
        return _

    lax.fori_loop(1, 8, ta_send, 0)
    TQ[zl] = TP[zl]

    def s2_copy(g, k):
        sl = Hb.at[g, :, x, c]
        return copy(sl, sl, s2s.at[g * 3 + k - 1], s2r.at[g * 3 + k - 1],
                    at_e(lax.rem(x + k, 4) * 2 + c))

    def s2_from(g, k):
        sl = Hb.at[g, :, lax.rem(x + 4 - k, 4), c]
        return copy(sl, sl, s2s.at[g * 3 + k - 1], s2r.at[g * 3 + k - 1],
                    at_e(lax.rem(x + k, 4) * 2 + c))

    def s3_copy(g):
        sl = Hb.at[g, :, :, c]
        return copy(sl, sl, s3s.at[g], s3r.at[g], sibling)

    def s3_from(g):
        sl = Hb.at[g, :, :, 1 - c]
        return copy(sl, sl, s3s.at[g], s3r.at[g], sibling)

    for g in (oh, h):
        def s1_wait(i, _):
            src = g * 8 + h * 4 + i

            @pl.when(src != z)
            def _go():
                sl = Hb.at[g, i, x, c]
                copy(hid_ref, sl, s1s.at[0], s1r.at[g * 4 + i], partner).wait_recv()
            return _

        lax.fori_loop(0, 4, s1_wait, 0)
        for k in (1, 3, 2):
            s2_copy(g, k).start()

    for g in (oh, h):
        for k in (1, 2, 3):
            s2_from(g, k).wait_recv()
        s3_copy(g).start()

    for g in (oh, h):
        s3_from(g).wait_recv()
        for i in range(4):
            blk = Hb[g, i].reshape(KS, TK)
            hh[g, :, i * KS:(i + 1) * KS] = blk.T

    def z_copy(ch):
        return copy(Sb.at[ch], Rb.at[ch], zs_.at[ch], zr_.at[ch], partner)

    def chunk(ch, _):
        w_wait_recv(ch)

        @pl.when(ch + 2 < NC)
        def _next():
            w_send(ch + 2)

        Sb[ch] = jnp.dot(hh[oh], Wc[ch], preferred_element_type=F32)
        z_copy(ch).start()
        L[ch] = jnp.dot(hh[h], Wc[ch], preferred_element_type=F32)
        return _

    lax.fori_loop(0, NC, chunk, 0)

    def ta_wait(k, _):
        frm = lax.rem(zl + 8 - k, 8)
        copy(TP.at[0], TQ.at[frm], tas.at[k - 1], tar.at[k - 1], partner).wait_recv()
        return _

    lax.fori_loop(1, 8, ta_wait, 0)
    for zz in range(8):
        rows = TQ[zz].astype(F32)
        for d in range(8):
            F2[d, 2 * zz:2 * zz + 2, :] = rows[2 * d:2 * d + 2]

    def tr_cast(d, _):
        TR[d] = F2[d].astype(BF16)
        return _

    lax.fori_loop(0, 8, tr_cast, 0)

    def tb_copy(k):
        to = lax.rem(e + k, 8)
        return copy(TR.at[to], TT.at[e], tbs.at[k - 1], tbr.at[k - 1], at_e(to))

    def tb_send(k, _):
        tb_copy(k).start()
        return _

    lax.fori_loop(1, 8, tb_send, 0)
    TT[e] = TR[e]

    def tb_wait(k, _):
        frm = lax.rem(e + 8 - k, 8)
        copy(TR.at[0], TT.at[frm], tbs.at[k - 1], tbr.at[k - 1], sibling).wait_recv()
        return _

    lax.fori_loop(1, 8, tb_wait, 0)

    lane = lax.broadcasted_iota(jnp.int32, (TK, VC), 1)
    low = F32(-3.0e38)

    def tea(ch):
        return TT[:, :, ch * VC:(ch + 1) * VC].reshape(TK, VC).astype(F32)

    m_s = jnp.full((TK, 1), low, F32)
    m_t = jnp.full((TK, 1), low, F32)
    for ch in range(NC):
        z_copy(ch).wait_recv()
        val = L[ch] + Rb[ch]
        L[ch] = val
        t = tea(ch)
        if ch == NC - 1:
            val = jnp.where(lane < tail, val, low)
            t = jnp.where(lane < tail, t, low)
        m_s = jnp.maximum(m_s, jnp.max(val, axis=1, keepdims=True))
        m_t = jnp.maximum(m_t, jnp.max(t, axis=1, keepdims=True))

    s_sum = jnp.zeros((TK, 1), F32)
    s_gap = jnp.zeros((TK, 1), F32)
    s_pick = jnp.zeros((TK, 1), F32)
    s_tea = jnp.zeros((TK, 1), F32)
    here = ids_ref[...] - v * VD
    for ch in range(NC):
        val = L[ch]
        t = tea(ch)
        ex = jnp.exp(val - m_s)
        et = jnp.exp(t - m_t)
        eg = ex * (val - t)
        pk = jnp.where(lane + ch * VC == here, val, 0.0)
        if ch == NC - 1:
            ok = lane < tail
            ex = jnp.where(ok, ex, 0.0)
            et = jnp.where(ok, et, 0.0)
            eg = jnp.where(ok, eg, 0.0)
            pk = jnp.where(ok, pk, 0.0)
        s_sum = s_sum + jnp.sum(ex, axis=1, keepdims=True)
        s_gap = s_gap + jnp.sum(eg, axis=1, keepdims=True)
        s_pick = s_pick + jnp.sum(pk, axis=1, keepdims=True)
        s_tea = s_tea + jnp.sum(et, axis=1, keepdims=True)

    sl = lax.broadcasted_iota(jnp.int32, (TK, 128), 1)
    pack_cols = jnp.zeros((TK, 128), F32)
    for n, col in enumerate((m_s, s_sum, s_gap, s_pick, m_t, s_tea)):
        pack_cols = jnp.where(sl == n, col, pack_cols)
    St[...] = pack_cols.T[0:8]

    def combine(ref):
        ms = ref[0, 0:1]
        mt = ref[0, 4:5]
        for j in range(1, 8):
            ms = jnp.maximum(ms, ref[j, 0:1])
            mt = jnp.maximum(mt, ref[j, 4:5])
        a = b = p = t = jnp.zeros((1, TK), F32)
        for j in range(8):
            f = jnp.exp(ref[j, 0:1] - ms)
            a = a + ref[j, 1:2] * f
            b = b + ref[j, 2:3] * f
            p = p + ref[j, 3:4]
            t = t + ref[j, 5:6] * jnp.exp(ref[j, 4:5] - mt)
        return ms, a, b, p, mt, t

    def sa_copy(k):
        return copy(St, StA.at[e], sas.at[k - 1], sar.at[k - 1], at_e(lax.rem(e + k, 8)))

    def sa_send(k, _):
        sa_copy(k).start()
        return _

    def sa_wait(k, _):
        copy(St, StA.at[lax.rem(e + 8 - k, 8)], sas.at[k - 1], sar.at[k - 1], sibling).wait_recv()
        return _

    lax.fori_loop(1, 8, sa_send, 0)
    StA[e] = St[...]
    lax.fori_loop(1, 8, sa_wait, 0)
    row = lax.broadcasted_iota(jnp.int32, (8, TK), 0)
    acc = jnp.zeros((8, TK), F32)
    for n, val in enumerate(combine(StA)):
        acc = jnp.where(row == n, val, acc)
    St2[...] = acc

    def sb_copy(k):
        return copy(St2, StB.at[zl], sbs.at[k - 1], sbr.at[k - 1], at_z(h * 8 + lax.rem(zl + k, 8)))

    def sb_send(k, _):
        sb_copy(k).start()
        return _

    def sb_wait(k, _):
        copy(St2, StB.at[lax.rem(zl + 8 - k, 8)], sbs.at[k - 1], sbr.at[k - 1], sibling).wait_recv()
        return _

    lax.fori_loop(1, 8, sb_send, 0)
    StB[zl] = St2[...]
    lax.fori_loop(1, 8, sb_wait, 0)
    ms, a, b, p, mt, t = combine(StB)
    s_lse = ms + jnp.log(a)
    t_lse = mt + jnp.log(t)
    div = b / a - s_lse + t_lse
    tok = jnp.zeros((8, TK), F32)
    for n, val in enumerate((div, p - s_lse, s_lse, t_lse)):
        tok = jnp.where(row == n, val, tok)
    tok_ref[...] = tok
    Zt[...] = jnp.zeros((128, TK), F32)
    Zt[0:8, :] = tok
    cols = Zt[...].T
    c_div = cols[:, 0:1]
    c_s = cols[:, 2:3]
    c_t = cols[:, 3:4]
    lw = lw_ref[...]

    def g_copy(ch):
        sl = GL.at[h, ch]
        return copy(sl, sl, gs.at[ch], gr.at[ch], partner)

    for ch in range(NC):
        val = L[ch]
        gl = lw * jnp.exp(val - c_s) * ((val - tea(ch)) - c_s + c_t - c_div)
        if ch == NC - 1:
            gl = jnp.where(lane < tail, gl, 0.0)
        GL[h, ch] = gl.astype(BF16)
        g_copy(ch).start()

    def c_copy(g):
        return copy(GT.at[g, :, :, 1 - c], RC.at[g], cs.at[g], cr.at[g], sibling)

    def x_copy(g, k):
        to = lax.rem(x + k, 4)
        return copy(X1.at[g, to], RX.at[g, k - 1], xs.at[g * 3 + k - 1], xr.at[g * 3 + k - 1],
                    at_e(to * 2 + c))

    def rz_copy(g, i):
        return copy(X2.at[g, i], RZ.at[zl], rzs.at[g * 4 + i], rzr.at[zl], at_z(g * 8 + h * 4 + i))

    for g in (h, oh):
        if g is oh:
            for ch in range(NC):
                sl = GL.at[oh, ch]
                copy(sl, sl, gs.at[ch], gr.at[ch], partner).wait_recv()

        def mm(i, _):
            for half in range(2):
                r0 = pl.multiple_of(i * KS + half * 320, 320)
                tot = jnp.zeros((320, TK), F32)
                for ch in range(NC):
                    tot = tot + lax.dot_general(
                        Wc[ch, pl.ds(r0, 320), :], GL[g, ch], (((1,), (1,)), ((), ())),
                        preferred_element_type=F32)
                GT[g, i, 2 * half:2 * half + 2] = tot.reshape(2, 2, OB, TK)
            return _

        lax.fori_loop(0, 4, mm, 0)
        c_copy(g).start()
        c_copy(g).wait_recv()

        def add_c(i, _):
            for xx in range(4):
                X1[g, xx, i] = GT[g, i, xx, c] + RC[g, i, xx]
            return _

        lax.fori_loop(0, 4, add_c, 0)
        for k in (1, 3, 2):
            x_copy(g, k).start()
        for k in (1, 2, 3):
            x_copy(g, k).wait_recv()

        def add_x(i, _):
            X2[g, i] = X1[g, x, i] + RX[g, 0, i] + RX[g, 1, i] + RX[g, 2, i]
            return _

        lax.fori_loop(0, 4, add_x, 0)

        def rz_send(i, _):
            dst = g * 8 + h * 4 + i

            @pl.when(dst != z)
            def _go():
                rz_copy(g, i).start()

            @pl.when(dst == z)
            def _own():
                RZ[zl] = X2[g, i]
            return _

        lax.fori_loop(0, 4, rz_send, 0)

    def rz_wait(k, _):
        @pl.when(hb * 8 + k != z)
        def _go():
            copy(X2.at[0, 0], RZ.at[k], rzs.at[0], rzr.at[k], partner).wait_recv()
        return _

    lax.fori_loop(0, 8, rz_wait, 0)
    tot = RZ[0]
    for k in range(1, 8):
        tot = tot + RZ[k]
    out_ref[...] = tot

    def s1_done(k, _):
        @pl.when(hb * 8 + k != z)
        def _go():
            feat_copy(k).wait_send()
        return _

    lax.fori_loop(0, 8, s1_done, 0)

    def w_done(ch, _):
        for k in (1, 2, 3):
            w_copy(ch, k).wait_send()
        z_copy(ch).wait_send()
        g_copy(ch).wait_send()
        return _

    lax.fori_loop(0, NC, w_done, 0)

    def p_done(k, _):
        ta_copy(k).wait_send()
        tb_copy(k).wait_send()
        sa_copy(k).wait_send()
        sb_copy(k).wait_send()
        return _

    lax.fori_loop(1, 8, p_done, 0)

    def g_done(g, _):
        for k in (1, 2, 3):
            s2_copy(g, k).wait_send()
            x_copy(g, k).wait_send()
        s3_copy(g).wait_send()
        c_copy(g).wait_send()
        for i in range(4):
            @pl.when(g * 8 + h * 4 + i != z)
            def _go():
                rz_copy(g, i).wait_send()
        return _

    lax.fori_loop(0, 2, g_done, 0)


def on_device(hidden, head_weight, teacher_logits, block_owner, sampled_ids, loss_weight):
    number = jnp.arange(64, dtype=jnp.int32)
    inv = jnp.sum(jnp.where(block_owner[None, :] == number[:, None], number[None, :], 0), axis=1).astype(jnp.int32)
    hid = hidden.reshape(8, 8, 2, OB).transpose(3, 1, 0, 2).reshape(OB, TK)
    ids = sampled_ids.reshape(8, 8, 2).transpose(1, 0, 2).reshape(TK, 1)
    lw = loss_weight.reshape(8, 8, 2).transpose(1, 0, 2).reshape(TK, 1)
    tea = teacher_logits.reshape(2, 64, VD).transpose(1, 0, 2).astype(F32)
    tea = jnp.pad(tea, ((0, 0), (0, 0), (0, VP - VD)))
    vm = pl.BlockSpec(memory_space=pltpu.VMEM)
    dma = pltpu.SemaphoreType.DMA
    out, tok = pl.pallas_call(
        kernel,
        out_shape=[jax.ShapeDtypeStruct((OB, TK), F32), jax.ShapeDtypeStruct((8, TK), F32)],
        in_specs=[pl.BlockSpec(memory_space=pltpu.SMEM)] + [vm] * 5,
        out_specs=[vm, vm],
        scratch_shapes=[
            pltpu.VMEM((2, 4, 4, 2, OB, TK), BF16),
            pltpu.VMEM((2, TK, KH), BF16),
            pltpu.VMEM((NC, KH, VC), BF16),
            pltpu.VMEM((NC, TK, VC), F32),
            pltpu.VMEM((NC, TK, VC), F32),
            pltpu.VMEM((NC, TK, VC), F32),
            pltpu.VMEM((16, VP), F32),
            pltpu.VMEM((8, 16, VP), BF16),
            pltpu.VMEM((8, 16, VP), BF16),
            pltpu.VMEM((8, 16, VP), F32),
            pltpu.VMEM((8, 16, VP), BF16),
            pltpu.VMEM((8, 16, VP), BF16),
            pltpu.VMEM((8, TK), F32),
            pltpu.VMEM((8, 8, TK), F32),
            pltpu.VMEM((8, TK), F32),
            pltpu.VMEM((8, 8, TK), F32),
            pltpu.VMEM((128, TK), F32),
            pltpu.VMEM((2, NC, TK, VC), BF16),
            pltpu.VMEM((2, 4, 4, 2, OB, TK), F32),
            pltpu.VMEM((2, 4, 4, OB, TK), F32),
            pltpu.VMEM((2, 4, 4, OB, TK), F32),
            pltpu.VMEM((2, 3, 4, OB, TK), F32),
            pltpu.VMEM((2, 4, OB, TK), F32),
            pltpu.VMEM((8, OB, TK), F32),
            dma((8,)), dma((8,)),
            dma((6,)), dma((6,)),
            dma((2,)), dma((2,)),
            dma((3 * NC,)), dma((3 * NC,)),
            dma((NC,)), dma((NC,)),
            dma((7,)), dma((7,)),
            dma((7,)), dma((7,)),
            dma((7,)), dma((7,)),
            dma((7,)), dma((7,)),
            dma((NC,)), dma((NC,)),
            dma((2,)), dma((2,)),
            dma((6,)), dma((6,)),
            dma((8,)), dma((8,)),
        ],
        compiler_params=pltpu.CompilerParams(
            collective_id=0, has_side_effects=True, vmem_limit_bytes=56 * 2**20
        ),
    )(inv, hid, head_weight, tea, ids, lw)
    grad = out.reshape(OB, 8, 8, 2).transpose(2, 1, 3, 0).reshape(TK, OB)
    tok = tok[0:2].reshape(2, 8, 8, 2).transpose(0, 2, 1, 3).reshape(2, TK)
    return grad, tok[0], tok[1]


def solution(mesh):
    return jax.shard_map(
        on_device,
        mesh=mesh,
        in_specs=(
            P("dp", "vocab"),
            P("dp", "vocab"),
            P(("dp", "vocab"), None),
            P(),
            P("dp"),
            P("dp"),
        ),
        out_specs=(P("dp", "vocab"), P("dp"), P("dp")),
        check_vma=False,
    )
```

time: 1420 us -> 194 us (0.14)
  the two profiles are of different devices: /device:TPU:16 before, /device:TPU:153 now
where the time goes in v1:
time: 194 us
  Pallas kernels  178 us (92%)
  local copies, waits for them, and re-layouts  12.7 us (7%)
  other arithmetic  2.53 us (1%)
    pallas_call x1, Pallas kernels, on_device(): pl.pallas_call(kernel, out_shape=[jax.ShapeDtypeStruct((OB, TK), F32), ja...  178 us

profile of v1, /device:TPU:153, one launch (start us, length us, event | category | flops | bytes accessed | tf_op | source)
XLA Modules:
  0.0 194.0 jit_solution(928415141566267760)
XLA Ops:
  0.6 0.0 copy-start
  0.6 1.4 select_reduce_fusion.inv_ref
  2.0 0.8 copy.31
  2.9 0.7 copy.36.hid_ref
  3.6 0.8 reshape.44
  4.4 0.7 reshape.51.ids_ref
  5.1 0.8 reshape.46
  5.9 0.7 reshape.52.lw_ref
  6.6 1.9 convert_element_type.9
  8.5 0.3 copy.46
  8.9 1.1 pad_convert_fusion.tea_ref
  10.0 0.0 copy-done
  10.0 2.2 %copy.37.w_ref = bf16[640,1188]{1,0:T(8,128)(2,1)} copy(bf16[640,1188]{0,1:T(8,128)(2,1)S(1)} %copy-done) | data formatting | bytes 3041280 | tf_op args[1]
  12.2 178.0 %shard_map.85 = (f32[80,128]{1,0:T(8,128)}, f32[8,128]{1,0:T(8,128)}) custom-call(s32[64]{0:T(128)} %select_reduce_fusion.inv_ref, bf16[80,128]{1,0:T(8,128)(2,1)} %copy.36.hid_ref, bf16[640,1188]{1,0:T(8,128)(2,1)} %copy.37.w_ref, f32[64,2,1280]{2,1,0:T(2,128)} %pad_convert_fusion.tea_ref, s32[128,1]{1,0:T(8,128)} %reshape.51.ids_ref, f32[128,1]{1,0:T(8,128)} %reshape.52.lw_ref), custom_call_target="tpu_custom_call" | custom-call | tf_op jit(solution)/shard_map/pallas_call | solution.py:483
  190.2 0.7 slice.11
  190.9 0.9 copy.40
  191.8 0.7 copy.44
  192.5 0.1 reshape.50
  192.7 0.7 squeeze.7
  193.4 0.7 squeeze.6
  (7 shorter events, 0.1 us)
Async XLA Ops:
  0.6 9.4 %copy-start = (bf16[640,1188]{0,1:T(8,128)(2,1)S(1)}, bf16[640,1188]{0,1:T(8,128)(2,1)}, u32[]{:S(2)}) copy-start(bf16[640,1188]{0,1:T(8,128)(2,1)} %param.7) | copy-start | bytes 4561924

commit v2 on v0

v2 whole, which is shorter than its diff:
```python
import jax
import jax.numpy as jnp
from jax import lax
from jax.experimental import pallas as pl
from jax.experimental.pallas import tpu as pltpu
from jax.sharding import PartitionSpec as P

MESH = pl.DeviceIdType.MESH
F32 = jnp.float32
BF16 = jnp.bfloat16

VD = 1188
VC = 240
NC = 5
VQ = VC * NC
VP = 1280
TAIL = VD - (NC - 1) * VC
KS = 640
KH = 4 * KS
TK = 128
OB = 80
WIN = VP + 128


def kernel(
    own_ref, hT, w_ref, tea_ref, ids_ref, lw_ref,
    out_ref,
    Wv, Ow, TJ, Hb, Wc, Sb, Rb, L, TP, TQ, TR, TT, TN,
    St, StA, St2, StB, GA, GL, GT, RC, X1, RX, X2, RQ, Qs, RZ,
    lds, s1s, s1r, s2s, s2r, s3s, s3r, ws, wr, fs, fr, zs_, zr_,
    tas, tar, tbs, tbr, sas, sar, sbs, sbr, gs, gr, cs, cr, xs, xr, rqs, rqr, rzs, rzr,
):
    dp = lax.axis_index("dp")
    v = lax.axis_index("vocab")
    h = lax.div(dp, 4)
    q = lax.rem(dp, 4)
    zl = lax.div(v, 8)
    e = lax.rem(v, 8)
    x = lax.div(e, 2)
    c = lax.rem(e, 2)
    z = h * 8 + zl
    oh = 1 - h
    hb = lax.div(zl, 4)
    ip = lax.rem(zl, 4)
    done = []

    def at_z(zz):
        return (lax.div(zz, 8) * 4 + q, lax.rem(zz, 8) * 8 + e)

    def at_y(yy):
        return (h * 4 + yy, v)

    def at_e(ee):
        return (dp, zl * 8 + ee)

    partner = at_z(oh * 8 + zl)
    sibling = at_e(x * 2 + 1 - c)

    def copy(src, dst, ss, rs, dev):
        return pltpu.make_async_remote_copy(
            src_ref=src, dst_ref=dst, send_sem=ss, recv_sem=rs, device_id=dev, device_id_type=MESH
        )

    def loop(lo, hi, body):
        def step(k, carry):
            body(k)
            return carry
        lax.fori_loop(lo, hi, step, 0)

    load_w = pltpu.make_async_copy(w_ref, Wv, lds)
    load_w.start()
    barrier = pltpu.get_barrier_semaphore()

    def greet(dev):
        pl.semaphore_signal(barrier, inc=1, device_id=dev, device_id_type=MESH)

    loop(1, 16, lambda k: greet(at_z(lax.rem(z + k, 16))))
    loop(1, 4, lambda k: greet(at_y(lax.rem(q + k, 4))))
    loop(1, 8, lambda k: greet(at_e(lax.rem(e + k, 8))))

    load_w.wait()
    full = VD // 16 * 16
    Wc[q, 0:full] = Wv[0:full]
    last = Wv[full:VD].astype(F32)
    Wc[q, full:VQ] = jnp.concatenate([last, jnp.zeros((VQ - VD, KS), F32)], axis=0).astype(BF16)

    def unpack(j):
        s = j * VD
        a = pl.multiple_of(jnp.minimum(lax.div(s, 128) * 128, 64 * VD - WIN), 128)
        win = tea_ref[:, pl.ds(a, WIN)].astype(F32)
        win = pltpu.roll(win, WIN - (s - a), 1)
        TJ[pl.ds(j, 1), :] = win[0:1, 0:VP]
        TJ[pl.ds(64 + j, 1), :] = win[1:2, 0:VP]

    loop(0, 64, unpack)
    Ow[:, 0:64] = own_ref[...]
    Ow[:, 64:128] = own_ref[...]
    r_i = lax.broadcasted_iota(jnp.int32, (128, 128), 0)
    c_i = lax.broadcasted_iota(jnp.int32, (128, 128), 1)

    def permute(mask, rows):
        return jnp.dot(mask.astype(F32).astype(BF16), rows, preferred_element_type=F32).astype(BF16)

    block = (r_i // 16) * 8 + r_i % 8
    pick = jnp.logical_and((r_i // 8) % 2 == c_i // 64, Ow[...] == block)
    TP[...] = permute(pick, TJ[...].astype(BF16)).reshape(8, 16, VP)

    pl.semaphore_wait(barrier, 25)

    def feat_copy(k):
        return copy(hT, Hb.at[h, ip, x, c], s1s.at[k], s1r.at[h * 4 + ip], at_z(hb * 8 + k))

    def not_self(k, fn):
        @pl.when(hb * 8 + k != z)
        def _go():
            fn(k)

    loop(0, 8, lambda k: not_self(k, lambda k: feat_copy(k).start()))
    done.append(lambda: loop(0, 8, lambda k: not_self(k, lambda k: feat_copy(k).wait_send())))

    @pl.when(hb == h)
    def _own():
        Hb[h, ip, x, c] = hT[...]

    def w_part(ch, yy, lo, n):
        rows = pl.ds(pl.multiple_of(ch * VC + lo, 16), n)
        return Wc.at[lax.rem(yy, 4), rows]

    HALF = (0, 128), (128, VC - 128)

    def w_copy(ch, k):
        sl = w_part(ch, q, 0, VC)
        n = ch * 2 + k // 2
        return copy(sl, sl, ws.at[n], wr.at[n], at_y(lax.rem(q + k, 4)))

    def w_from(ch, k):
        sl = w_part(ch, q + 4 - k, 0, VC)
        n = ch * 2 + k // 2
        return copy(sl, sl, ws.at[n], wr.at[n], partner)

    def f_copy(ch, k):
        sl = w_part(ch, q + 4 - k, *HALF[k // 2])
        n = ch * 2 + k // 2
        return copy(sl, sl, fs.at[n], fr.at[n], at_y(lax.rem(q + k, 4)))

    def f_from(ch, k):
        sl = w_part(ch, q + 2, *HALF[k // 2])
        n = ch * 2 + k // 2
        return copy(sl, sl, fs.at[n], fr.at[n], partner)

    def w_send(ch):
        for k in (1, 3):
            w_copy(ch, k).start()

    def w_pass(ch):
        for k in (1, 3):
            w_from(ch, k).wait_recv()
            f_copy(ch, k).start()

        @pl.when(ch + 1 < NC)
        def _more():
            w_send(ch + 1)

    def w_done(ch):
        for k in (1, 3):
            w_copy(ch, k).wait_send()
            f_copy(ch, k).wait_send()

    w_send(0)
    done.append(lambda: loop(0, NC, w_done))

    def s2_copy(g, k):
        sl = Hb.at[g, :, x, c]
        return copy(sl, sl, s2s.at[g * 3 + k - 1], s2r.at[g * 3 + k - 1],
                    at_e(lax.rem(x + k, 4) * 2 + c))

    def s2_from(g, k):
        sl = Hb.at[g, :, lax.rem(x + 4 - k, 4), c]
        return copy(sl, sl, s2s.at[g * 3 + k - 1], s2r.at[g * 3 + k - 1], partner)

    def s3_copy(g):
        sl = Hb.at[g, :, :, c]
        return copy(sl, sl, s3s.at[g], s3r.at[g], sibling)

    def s3_from(g):
        sl = Hb.at[g, :, :, 1 - c]
        return copy(sl, sl, s3s.at[g], s3r.at[g], sibling)

    for g in (oh, h):
        def s1_wait(i):
            @pl.when(g * 8 + h * 4 + i != z)
            def _go():
                copy(hT, Hb.at[g, i, x, c], s1s.at[0], s1r.at[g * 4 + i], partner).wait_recv()

        loop(0, 4, s1_wait)
        for k in (1, 3, 2):
            s2_copy(g, k).start()

    def ta_copy(k):
        to = lax.rem(zl + k, 8)
        return copy(TP.at[to], TQ.at[zl], tas.at[k - 1], tar.at[k - 1], at_z(h * 8 + to))

    loop(1, 8, lambda k: ta_copy(k).start())
    done.append(lambda: loop(1, 8, lambda k: ta_copy(k).wait_send()))
    TQ[zl] = TP[zl]

    w_pass(0)
    for g in (oh, h):
        for k in (1, 3, 2):
            s2_from(g, k).wait_recv()
        s3_copy(g).start()
    w_pass(1)
    s3_from(oh).wait_recv()

    def s_done(g):
        for k in (1, 2, 3):
            s2_copy(g, k).wait_send()
        s3_copy(g).wait_send()

    done.append(lambda: loop(0, 2, s_done))

    def z_copy(ch):
        return copy(Sb.at[ch], Rb.at[ch], zs_.at[ch], zr_.at[ch], partner)

    def rows_of(ch):
        return pl.ds(pl.multiple_of(ch * VC, 16), VC)

    def part(g, ch):
        tot = None
        for i in range(4):
            one = jnp.dot(Wc[i, rows_of(ch)], Hb[g, i].reshape(KS, TK), preferred_element_type=F32)
            tot = one if tot is None else tot + one
        return tot

    def chunk(ch):
        for k in (1, 3):
            f_from(ch, k).wait_recv()
        Sb[ch] = part(oh, ch)
        z_copy(ch).start()

        @pl.when(ch + 2 < NC)
        def _next():
            w_pass(ch + 2)

        @pl.when(ch == 0)
        def _feat():
            s3_from(h).wait_recv()

        L[ch] = part(h, ch)

    loop(0, NC, chunk)
    done.append(lambda: loop(0, NC, lambda ch: z_copy(ch).wait_send()))

    def ta_wait(k):
        frm = lax.rem(zl + 8 - k, 8)
        copy(TP.at[0], TQ.at[frm], tas.at[k - 1], tar.at[k - 1], partner).wait_recv()

    loop(1, 8, ta_wait)
    pick = jnp.logical_and(
        r_i // 16 == c_i % 8,
        jnp.logical_and((r_i // 2) % 8 == c_i // 16, r_i % 2 == (c_i // 8) % 2))
    TR[...] = permute(pick, TQ[...].reshape(TK, VP)).reshape(8, 16, VP)

    def tb_copy(k):
        to = lax.rem(e + k, 8)
        return copy(TR.at[to], TT.at[e], tbs.at[k - 1], tbr.at[k - 1], at_e(to))

    def tb_wait(k):
        frm = lax.rem(e + 8 - k, 8)
        copy(TR.at[0], TT.at[frm], tbs.at[k - 1], tbr.at[k - 1], sibling).wait_recv()

    loop(1, 8, lambda k: tb_copy(k).start())
    done.append(lambda: loop(1, 8, lambda k: tb_copy(k).wait_send()))
    TT[e] = TR[e]
    here = ids_ref[...] - v * VD
    lw = lw_ref[...]
    loop(1, 8, tb_wait)
    pick = jnp.logical_and(
        c_i // 16 == (r_i // 2) % 8,
        jnp.logical_and((c_i // 2) % 8 == r_i // 16, c_i % 2 == r_i % 2))
    TN[...] = lax.dot_general(
        TT[...].reshape(TK, VP), pick.astype(F32).astype(BF16), (((0,), (0,)), ((), ())),
        preferred_element_type=F32)

    lane = lax.broadcasted_iota(jnp.int32, (VC, TK), 0)
    low = F32(-3.0e38)

    def tea(ch):
        return TN[ch * VC:(ch + 1) * VC, :]

    m_s = jnp.full((1, TK), low, F32)
    m_t = jnp.full((1, TK), low, F32)
    for ch in range(NC):
        z_copy(ch).wait_recv()
        val = L[ch] + Rb[ch]
        L[ch] = val
        t = tea(ch)
        if ch == NC - 1:
            val = jnp.where(lane < TAIL, val, low)
            t = jnp.where(lane < TAIL, t, low)
        m_s = jnp.maximum(m_s, jnp.max(val, axis=0, keepdims=True))
        m_t = jnp.maximum(m_t, jnp.max(t, axis=0, keepdims=True))

    s_sum = jnp.zeros((1, TK), F32)
    s_gap = jnp.zeros((1, TK), F32)
    s_pick = jnp.zeros((1, TK), F32)
    s_tea = jnp.zeros((1, TK), F32)
    for ch in range(NC):
        val = L[ch]
        t = tea(ch)
        ex = jnp.exp(val - m_s)
        et = jnp.exp(t - m_t)
        eg = ex * (val - t)
        pk = jnp.where(lane + ch * VC == here, val, 0.0)
        if ch == NC - 1:
            ok = lane < TAIL
            ex = jnp.where(ok, ex, 0.0)
            et = jnp.where(ok, et, 0.0)
            eg = jnp.where(ok, eg, 0.0)
            pk = jnp.where(ok, pk, 0.0)
        s_sum = s_sum + jnp.sum(ex, axis=0, keepdims=True)
        s_gap = s_gap + jnp.sum(eg, axis=0, keepdims=True)
        s_pick = s_pick + jnp.sum(pk, axis=0, keepdims=True)
        s_tea = s_tea + jnp.sum(et, axis=0, keepdims=True)

    row = lax.broadcasted_iota(jnp.int32, (8, TK), 0)

    def stack(vals):
        acc = jnp.zeros((8, TK), F32)
        for n, val in enumerate(vals):
            acc = jnp.where(row == n, val, acc)
        return acc

    St[...] = stack((m_s, s_sum, s_gap, s_pick, m_t, s_tea))

    def combine(ref):
        ms = ref[0, 0:1]
        mt = ref[0, 4:5]
        for j in range(1, 8):
            ms = jnp.maximum(ms, ref[j, 0:1])
            mt = jnp.maximum(mt, ref[j, 4:5])
        a = b = p = t = jnp.zeros((1, TK), F32)
        for j in range(8):
            f = jnp.exp(ref[j, 0:1] - ms)
            a = a + ref[j, 1:2] * f
            b = b + ref[j, 2:3] * f
            p = p + ref[j, 3:4]
            t = t + ref[j, 5:6] * jnp.exp(ref[j, 4:5] - mt)
        return ms, a, b, p, mt, t

    def sa_copy(k):
        return copy(St, StA.at[e], sas.at[k - 1], sar.at[k - 1], at_e(lax.rem(e + k, 8)))

    def sa_wait(k):
        copy(St, StA.at[lax.rem(e + 8 - k, 8)], sas.at[k - 1], sar.at[k - 1], sibling).wait_recv()

    loop(1, 8, lambda k: sa_copy(k).start())
    done.append(lambda: loop(1, 8, lambda k: sa_copy(k).wait_send()))
    StA[e] = St[...]
    loop(1, 8, sa_wait)
    St2[...] = stack(combine(StA))

    def sb_copy(k):
        return copy(St2, StB.at[zl], sbs.at[k - 1], sbr.at[k - 1], at_z(h * 8 + lax.rem(zl + k, 8)))

    def sb_wait(k):
        copy(St2, StB.at[lax.rem(zl + 8 - k, 8)], sbs.at[k - 1], sbr.at[k - 1], sibling).wait_recv()

    loop(1, 8, lambda k: sb_copy(k).start())
    done.append(lambda: loop(1, 8, lambda k: sb_copy(k).wait_send()))
    StB[zl] = St2[...]
    loop(1, 8, sb_wait)
    ms, a, b, p, mt, t = combine(StB)
    s_lse = ms + jnp.log(a)
    t_lse = mt + jnp.log(t)
    div = b / a - s_lse + t_lse
    out_ref[OB:OB + 8, :] = stack((div, p - s_lse))

    def g_copy(ch):
        sl = GL.at[h, ch]
        return copy(sl, sl, gs.at[ch], gr.at[ch], partner)

    def g_wait(ch):
        sl = GL.at[oh, ch]
        copy(sl, sl, gs.at[ch], gr.at[ch], partner).wait_recv()

    for ch in range(NC):
        val = L[ch]
        gl = lw * jnp.exp(val - s_lse) * ((val - tea(ch)) - s_lse + t_lse - div)
        if ch == NC - 1:
            gl = jnp.where(lane < TAIL, gl, 0.0)
        GL[h, ch] = gl.astype(BF16)
        g_copy(ch).start()
    done.append(lambda: loop(0, NC, lambda ch: g_copy(ch).wait_send()))
    def c_copy(g, i):
        n = g * 4 + i
        return copy(GT.at[g, i, :, 1 - c], RC.at[g, i], cs.at[n], cr.at[n], sibling)

    def x_copy(g, i, k):
        to = lax.rem(x + k, 4)
        n = (g * 4 + i) * 3 + k - 1
        return copy(X1.at[g, i, to], RX.at[g, i, k - 1], xs.at[n], xr.at[n], at_e(to * 2 + c))

    def rq_copy(g, i):
        return copy(X2.at[g, i], RQ.at[g, ip], rqs.at[g * 4 + i], rqr.at[g * 4 + ip],
                    at_z(h * 8 + hb * 4 + i))

    def rz_copy(g):
        return copy(Qs.at[g], RZ.at[hb], rzs.at[g], rzr.at[hb], at_z(g * 8 + h * 4 + ip))

    def x_stage(g, i):
        c_copy(g, i).wait_recv()
        for xx in range(4):
            X1[g, i, xx] = GT[g, i, xx, c] + RC[g, i, xx]
        for k in (2, 1, 3):
            x_copy(g, i, k).start()

    def x_sum(g, i):
        for k in (1, 3, 2):
            x_copy(g, i, k).wait_recv()
        X2[g, i] = X1[g, i, x] + RX[g, i, 0] + RX[g, i, 1] + RX[g, i, 2]

    def not_me(i, fn):
        @pl.when(i != ip)
        def _go():
            fn()

    def q_stage(g, i):
        not_me(i, lambda: rq_copy(g, i).start())

        @pl.when(i == ip)
        def _own():
            RQ[g, ip] = X2[g, i]

    def z_stage(g):
        def q_wait(i):
            not_me(i, lambda: copy(
                X2.at[g, 0], RQ.at[g, i], rqs.at[0], rqr.at[g * 4 + i], partner).wait_recv())

        loop(0, 4, q_wait)
        Qs[g] = RQ[g, 0] + RQ[g, 1] + RQ[g, 2] + RQ[g, 3]
        dst = g * 8 + h * 4 + ip

        @pl.when(dst != z)
        def _go():
            rz_copy(g).start()

        @pl.when(dst == z)
        def _own():
            RZ[hb] = Qs[g]

    def mm(g, i, chs):
        tot = None
        for ch in chs:
            one = lax.dot_general(
                GL[g, ch], Wc[i, ch * VC:(ch + 1) * VC],
                (((0,), (0,)), ((), ())), preferred_element_type=F32)
            tot = one if tot is None else tot + one
        return tot

    def to_send(g, i, tot):
        GT[g, i] = tot.T.reshape(4, 2, OB, TK)
        c_copy(g, i).start()

    def own_mm(i):
        to_send(h, i, mm(h, i, range(NC)))

    loop(0, 4, own_mm)
    loop(0, 4, lambda i: x_stage(h, i))
    loop(0, 4, lambda i: x_sum(h, i))

    g_wait(0)
    g_wait(1)

    def oth_a(i):
        GA[i] = mm(oh, i, (0, 1))

    def oth_b(i):
        GA[i] = GA[i] + mm(oh, i, (2, 3))

    def oth_c(i):
        to_send(oh, i, GA[i] + mm(oh, i, (4,)))

    loop(0, 4, oth_a)
    g_wait(2)
    g_wait(3)
    loop(0, 4, oth_b)
    g_wait(4)
    loop(0, 4, lambda i: q_stage(h, i))
    loop(0, 4, oth_c)
    loop(0, 4, lambda i: x_stage(oh, i))
    z_stage(h)

    def tail(i):
        x_sum(oh, i)
        q_stage(oh, i)

    loop(0, 4, tail)
    z_stage(oh)

    def rz_wait(r):
        @pl.when(hb * 8 + r * 4 + ip != z)
        def _go():
            copy(Qs.at[0], RZ.at[r], rzs.at[0], rzr.at[r], partner).wait_recv()

    loop(0, 2, rz_wait)
    out_ref[0:OB, :] = RZ[0] + RZ[1]

    def rs_done(n):
        g = lax.div(n, 4)
        i = lax.rem(n, 4)
        c_copy(g, i).wait_send()
        for k in (1, 2, 3):
            x_copy(g, i, k).wait_send()

        not_me(i, lambda: rq_copy(g, i).wait_send())

    def rz_done(g):
        @pl.when(g * 8 + h * 4 + ip != z)
        def _go():
            rz_copy(g).wait_send()

    done.append(lambda: loop(0, 8, rs_done))
    done.append(lambda: loop(0, 2, rz_done))

    for fn in done:
        fn()


def split(both_ref, grad_ref, div_ref, slp_ref):
    grad_ref[...] = both_ref[0:OB, :]
    div_ref[...] = both_ref[OB:OB + 1, :]
    slp_ref[...] = both_ref[OB + 1:OB + 2, :]


def on_device(hidden, head_weight, teacher_logits, block_owner, sampled_ids, loss_weight):
    vm = pl.BlockSpec(memory_space=pltpu.VMEM)
    dma = pltpu.SemaphoreType.DMA
    both = pl.pallas_call(
        kernel,
        out_shape=jax.ShapeDtypeStruct((OB + 8, TK), F32),
        in_specs=[vm, vm, pl.BlockSpec(memory_space=pl.ANY), vm, vm, vm],
        out_specs=vm,
        scratch_shapes=[
            pltpu.VMEM((VD, KS), BF16),
            pltpu.VMEM((1, 128), jnp.int32),
            pltpu.VMEM((128, VP), F32),
            pltpu.VMEM((2, 4, 4, 2, OB, TK), BF16),
            pltpu.VMEM((4, VQ, KS), BF16),
            pltpu.VMEM((NC, VC, TK), F32),
            pltpu.VMEM((NC, VC, TK), F32),
            pltpu.VMEM((NC, VC, TK), F32),
            pltpu.VMEM((8, 16, VP), BF16),
            pltpu.VMEM((8, 16, VP), BF16),
            pltpu.VMEM((8, 16, VP), BF16),
            pltpu.VMEM((8, 16, VP), BF16),
            pltpu.VMEM((VP, TK), F32),
            pltpu.VMEM((8, TK), F32),
            pltpu.VMEM((8, 8, TK), F32),
            pltpu.VMEM((8, TK), F32),
            pltpu.VMEM((8, 8, TK), F32),
            pltpu.VMEM((4, TK, KS), F32),
            pltpu.VMEM((2, NC, VC, TK), BF16),
            pltpu.VMEM((2, 4, 4, 2, OB, TK), F32),
            pltpu.VMEM((2, 4, 4, OB, TK), F32),
            pltpu.VMEM((2, 4, 4, OB, TK), F32),
            pltpu.VMEM((2, 4, 3, OB, TK), F32),
            pltpu.VMEM((2, 4, OB, TK), F32),
            pltpu.VMEM((2, 4, OB, TK), F32),
            pltpu.VMEM((2, OB, TK), F32),
            pltpu.VMEM((2, OB, TK), F32),
            dma,
            dma((8,)), dma((8,)),
            dma((6,)), dma((6,)),
            dma((2,)), dma((2,)),
            dma((2 * NC,)), dma((2 * NC,)),
            dma((2 * NC,)), dma((2 * NC,)),
            dma((NC,)), dma((NC,)),
            dma((7,)), dma((7,)),
            dma((7,)), dma((7,)),
            dma((7,)), dma((7,)),
            dma((7,)), dma((7,)),
            dma((NC,)), dma((NC,)),
            dma((8,)), dma((8,)),
            dma((24,)), dma((24,)),
            dma((8,)), dma((8,)),
            dma((2,)), dma((2,)),
        ],
        compiler_params=pltpu.CompilerParams(
            collective_id=0, has_side_effects=True, vmem_limit_bytes=56 * 2**20
        ),
    )(block_owner.reshape(1, 64), hidden.T, head_weight.T, teacher_logits,
      sampled_ids.reshape(1, TK), loss_weight.reshape(1, TK))
    grad, div, slp = pl.pallas_call(
        split,
        out_shape=[
            jax.ShapeDtypeStruct((OB, TK), F32),
            jax.ShapeDtypeStruct((1, TK), F32),
            jax.ShapeDtypeStruct((1, TK), F32),
        ],
        in_specs=[vm],
        out_specs=[vm, vm, vm],
    )(both)
    return grad.T, div.reshape(TK), slp.reshape(TK)


def solution(mesh):
    return jax.shard_map(
        on_device,
        mesh=mesh,
        in_specs=(
            P("dp", "vocab"),
            P("dp", "vocab"),
            P(("dp", "vocab"), None),
            P(),
            P("dp"),
            P("dp"),
        ),
        out_specs=(P("dp", "vocab"), P("dp"), P("dp")),
        check_vma=False,
    )
```

time: 1420 us -> 166 us (0.12)
  the two profiles are of different devices: /device:TPU:16 before, /device:TPU:360 now
where the time goes in v2:
time: 166 us
  Pallas kernels  165 us (99%)
    pallas_call x1, Pallas kernels, on_device(): pl.pallas_call(kernel, out_shape=jax.ShapeDtypeStruct((OB + 8, TK), F32),...  164 us

profile of v2, /device:TPU:360, one launch (start us, length us, event | category | flops | bytes accessed | tf_op | source)
XLA Modules:
  0.0 166.0 jit_solution(13189494539396886182)
XLA Ops:
  0.6 163.9 %shard_map.85.both_ref = f32[88,128]{1,0:T(8,128)} custom-call(s32[1,64]{1,0:T(1,128)} %bitcast.10, bf16[80,128]{1,0:T(8,128)(2,1)} %bitcast.9, bf16[1188,640]{1,0:T(8,128)(2,1)} %bitcast.8, bf16[2,76032]{1,0:T(2,128)(2,1)} %tea_ref.1, s32[1,128]{1,0:T(1,128)} %bitcast.11, f32[1,128]{1,0:T(1,128)} %bitcast.12), custom_call_target="tpu_custom_call" | custom-call | tf_op jit(solution)/shard_map/pallas_call | solution.py:539
  164.5 1.4 shard_map.86

commit v3 on v2

--- a/solution.py
+++ b/solution.py
@@ -25,9 +25,9 @@
 def kernel(
     own_ref, hT, w_ref, tea_ref, ids_ref, lw_ref,
     out_ref,
-    Wv, Ow, TJ, Hb, Wc, Sb, Rb, L, TP, TQ, TR, TT, TN,
+    Wv, Tv, Ow, TJ, Hb, Wc, Sb, Rb, L, TP, TQ, TR, TT, TN,
     St, StA, St2, StB, GA, GL, GT, RC, X1, RX, X2, RQ, Qs, RZ,
-    lds, s1s, s1r, s2s, s2r, s3s, s3r, ws, wr, fs, fr, zs_, zr_,
+    lds, ldt, s1s, s1r, s2s, s2r, s3s, s3r, ws, wr, fs, fr, zs_, zr_,
     tas, tar, tbs, tbr, sas, sar, sbs, sbr, gs, gr, cs, cr, xs, xr, rqs, rqr, rzs, rzr,
 ):
     dp = lax.axis_index("dp")
@@ -69,6 +69,8 @@
 
     load_w = pltpu.make_async_copy(w_ref, Wv, lds)
     load_w.start()
+    load_t = pltpu.make_async_copy(tea_ref, Tv, ldt)
+    load_t.start()
     barrier = pltpu.get_barrier_semaphore()
 
     def greet(dev):
@@ -77,6 +79,23 @@
     loop(1, 16, lambda k: greet(at_z(lax.rem(z + k, 16))))
     loop(1, 4, lambda k: greet(at_y(lax.rem(q + k, 4))))
     loop(1, 8, lambda k: greet(at_e(lax.rem(e + k, 8))))
+
+    pl.semaphore_wait(barrier, 25)
+
+    def feat_copy(k):
+        return copy(hT, Hb.at[h, ip, x, c], s1s.at[k], s1r.at[h * 4 + ip], at_z(hb * 8 + k))
+
+    def not_self(k, fn):
+        @pl.when(hb * 8 + k != z)
+        def _go():
+            fn(k)
+
+    loop(0, 8, lambda k: not_self(k, lambda k: feat_copy(k).start()))
+    done.append(lambda: loop(0, 8, lambda k: not_self(k, lambda k: feat_copy(k).wait_send())))
+
+    @pl.when(hb == h)
+    def _own():
+        Hb[h, ip, x, c] = hT[...]
 
     load_w.wait()
     full = VD // 16 * 16
@@ -84,10 +103,61 @@
     last = Wv[full:VD].astype(F32)
     Wc[q, full:VQ] = jnp.concatenate([last, jnp.zeros((VQ - VD, KS), F32)], axis=0).astype(BF16)
 
+
+    def w_part(ch, yy, lo, n):
+        rows = pl.ds(pl.multiple_of(ch * VC + lo, 16), n)
+        return Wc.at[lax.rem(yy, 4), rows]
+
+    HALF = (0, 128), (128, VC - 128)
+
+    def w_copy(ch, k):
+        sl = w_part(ch, q, 0, VC)
+        n = ch * 2 + k // 2
+        return copy(sl, sl, ws.at[n], wr.at[n], at_y(lax.rem(q + k, 4)))
+
+    def w_from(ch, k):
+        sl = w_part(ch, q + 4 - k, 0, VC)
+        n = ch * 2 + k // 2
+        return copy(sl, sl, ws.at[n], wr.at[n], partner)
+
+    def f_copy(ch, k):
+        sl = w_part(ch, q + 4 - k, *HALF[k // 2])
+        n = ch * 2 + k // 2
+        return copy(sl, sl, fs.at[n], fr.at[n], at_y(lax.rem(q + k, 4)))
+
+    def f_from(ch, k):
+        sl = w_part(ch, q + 2, *HALF[k // 2])
+        n = ch * 2 + k // 2
+        return copy(sl, sl, fs.at[n], fr.at[n], partner)
+
+    def w_send(ch):
+        for k in (1, 3):
+            w_copy(ch, k).start()
+
+    def w_pass(ch):
+        for k in (1, 3):
+            w_from(ch, k).wait_recv()
+            f_copy(ch, k).start()
+
+        @pl.when(ch + 2 < NC)
+        def _more():
+            w_send(ch + 2)
+
+    def w_done(ch):
+        for k in (1, 3):
+            w_copy(ch, k).wait_send()
+            f_copy(ch, k).wait_send()
+
+    w_send(0)
+    w_send(1)
+    done.append(lambda: loop(0, NC, w_done))
+
+    load_t.wait()
+
     def unpack(j):
         s = j * VD
         a = pl.multiple_of(jnp.minimum(lax.div(s, 128) * 128, 64 * VD - WIN), 128)
-        win = tea_ref[:, pl.ds(a, WIN)].astype(F32)
+        win = Tv[:, pl.ds(a, WIN)].astype(F32)
         win = pltpu.roll(win, WIN - (s - a), 1)
         TJ[pl.ds(j, 1), :] = win[0:1, 0:VP]
         TJ[pl.ds(64 + j, 1), :] = win[1:2, 0:VP]
@@ -105,69 +175,13 @@
     pick = jnp.logical_and((r_i // 8) % 2 == c_i // 64, Ow[...] == block)
     TP[...] = permute(pick, TJ[...].astype(BF16)).reshape(8, 16, VP)
 
-    pl.semaphore_wait(barrier, 25)
-
-    def feat_copy(k):
-        return copy(hT, Hb.at[h, ip, x, c], s1s.at[k], s1r.at[h * 4 + ip], at_z(hb * 8 + k))
-
-    def not_self(k, fn):
-        @pl.when(hb * 8 + k != z)
-        def _go():
-            fn(k)
-
-    loop(0, 8, lambda k: not_self(k, lambda k: feat_copy(k).start()))
-    done.append(lambda: loop(0, 8, lambda k: not_self(k, lambda k: feat_copy(k).wait_send())))
-
-    @pl.when(hb == h)
-    def _own():
-        Hb[h, ip, x, c] = hT[...]
-
-    def w_part(ch, yy, lo, n):
-        rows = pl.ds(pl.multiple_of(ch * VC + lo, 16), n)
-        return Wc.at[lax.rem(yy, 4), rows]
-
-    HALF = (0, 128), (128, VC - 128)
-
-    def w_copy(ch, k):
-        sl = w_part(ch, q, 0, VC)
-        n = ch * 2 + k // 2
-        return copy(sl, sl, ws.at[n], wr.at[n], at_y(lax.rem(q + k, 4)))
-
-    def w_from(ch, k):
-        sl = w_part(ch, q + 4 - k, 0, VC)
-        n = ch * 2 + k // 2
-        return copy(sl, sl, ws.at[n], wr.at[n], partner)
-
-    def f_copy(ch, k):
-        sl = w_part(ch, q + 4 - k, *HALF[k // 2])
-        n = ch * 2 + k // 2
-        return copy(sl, sl, fs.at[n], fr.at[n], at_y(lax.rem(q + k, 4)))
-
-    def f_from(ch, k):
-        sl = w_part(ch, q + 2, *HALF[k // 2])
-        n = ch * 2 + k // 2
-        return copy(sl, sl, fs.at[n], fr.at[n], partner)
-
-    def w_send(ch):
-        for k in (1, 3):
-            w_copy(ch, k).start()
-
-    def w_pass(ch):
-        for k in (1, 3):
-            w_from(ch, k).wait_recv()
-            f_copy(ch, k).start()
-
-        @pl.when(ch + 1 < NC)
-        def _more():
-            w_send(ch + 1)
-
-    def w_done(ch):
-        for k in (1, 3):
-            w_copy(ch, k).wait_send()
-            f_copy(ch, k).wait_send()
-
-    w_send(0)
-    done.append(lambda: loop(0, NC, w_done))
+    def ta_copy(k):
+        to = lax.rem(zl + k, 8)
+        return copy(TP.at[to], TQ.at[zl], tas.at[k - 1], tar.at[k - 1], at_z(h * 8 + to))
+
+    loop(1, 8, lambda k: ta_copy(k).start())
+    done.append(lambda: loop(1, 8, lambda k: ta_copy(k).wait_send()))
+    TQ[zl] = TP[zl]
 
     def s2_copy(g, k):
         sl = Hb.at[g, :, x, c]
@@ -195,14 +209,6 @@
         loop(0, 4, s1_wait)
         for k in (1, 3, 2):
             s2_copy(g, k).start()
-
-    def ta_copy(k):
-        to = lax.rem(zl + k, 8)
-        return copy(TP.at[to], TQ.at[zl], tas.at[k - 1], tar.at[k - 1], at_z(h * 8 + to))
-
-    loop(1, 8, lambda k: ta_copy(k).start())
-    done.append(lambda: loop(1, 8, lambda k: ta_copy(k).wait_send()))
-    TQ[zl] = TP[zl]
 
     w_pass(0)
     for g in (oh, h):
@@ -391,7 +397,6 @@
             gl = jnp.where(lane < TAIL, gl, 0.0)
         GL[h, ch] = gl.astype(BF16)
         g_copy(ch).start()
-    done.append(lambda: loop(0, NC, lambda ch: g_copy(ch).wait_send()))
     def c_copy(g, i):
         n = g * 4 + i
         return copy(GT.at[g, i, :, 1 - c], RC.at[g, i], cs.at[n], cr.at[n], sibling)
@@ -485,9 +490,20 @@
     g_wait(2)
     g_wait(3)
     loop(0, 4, oth_b)
+    def cx_done(g, i):
+        c_copy(g, i).wait_send()
+        for k in (1, 2, 3):
+            x_copy(g, i, k).wait_send()
+
+    loop(0, 4, lambda i: cx_done(h, i))
     g_wait(4)
+
+    def last(i):
+        oth_c(i)
+
+
     loop(0, 4, lambda i: q_stage(h, i))
-    loop(0, 4, oth_c)
+    loop(0, 4, last)
     loop(0, 4, lambda i: x_stage(oh, i))
     z_stage(h)
 
@@ -497,6 +513,16 @@
 
     loop(0, 4, tail)
     z_stage(oh)
+    for fn in done:
+        fn()
+    loop(0, NC, lambda ch: g_copy(ch).wait_send())
+
+    def q_done(i):
+        cx_done(oh, i)
+        for g in range(2):
+            not_me(i, lambda: rq_copy(g, i).wait_send())
+
+    loop(0, 4, q_done)
 
     def rz_wait(r):
         @pl.when(hb * 8 + r * 4 + ip != z)
@@ -506,25 +532,10 @@
     loop(0, 2, rz_wait)
     out_ref[0:OB, :] = RZ[0] + RZ[1]
 
-    def rs_done(n):
-        g = lax.div(n, 4)
-        i = lax.rem(n, 4)
-        c_copy(g, i).wait_send()
-        for k in (1, 2, 3):
-            x_copy(g, i, k).wait_send()
-
-        not_me(i, lambda: rq_copy(g, i).wait_send())
-
-    def rz_done(g):
+    for g in range(2):
         @pl.when(g * 8 + h * 4 + ip != z)
-        def _go():
+        def _left():
             rz_copy(g).wait_send()
-
-    done.append(lambda: loop(0, 8, rs_done))
-    done.append(lambda: loop(0, 2, rz_done))
-
-    for fn in done:
-        fn()
 
 
 def split(both_ref, grad_ref, div_ref, slp_ref):
@@ -539,10 +550,11 @@
     both = pl.pallas_call(
         kernel,
         out_shape=jax.ShapeDtypeStruct((OB + 8, TK), F32),
-        in_specs=[vm, vm, pl.BlockSpec(memory_space=pl.ANY), vm, vm, vm],
+        in_specs=[vm, vm, pl.BlockSpec(memory_space=pl.ANY), pl.BlockSpec(memory_space=pl.ANY), vm, vm],
         out_specs=vm,
         scratch_shapes=[
             pltpu.VMEM((VD, KS), BF16),
+            pltpu.VMEM((2, 64 * VD), BF16),
             pltpu.VMEM((1, 128), jnp.int32),
             pltpu.VMEM((128, VP), F32),
             pltpu.VMEM((2, 4, 4, 2, OB, TK), BF16),
@@ -569,7 +581,7 @@
             pltpu.VMEM((2, 4, OB, TK), F32),
             pltpu.VMEM((2, OB, TK), F32),
             pltpu.VMEM((2, OB, TK), F32),
-            dma,
+            dma, dma,
             dma((8,)), dma((8,)),
             dma((6,)), dma((6,)),
             dma((2,)), dma((2,)),

time: 166 us -> 161 us (0.970)
  the two profiles are of different devices: /device:TPU:360 before, /device:TPU:160 now
where the time goes in v3:
time: 161 us
  Pallas kernels  160 us (99%)
    pallas_call x1, Pallas kernels, on_device(): pl.pallas_call(kernel, out_shape=jax.ShapeDtypeStruct((OB + 8, TK), F32),...  159 us

profile of v3, /device:TPU:160, one launch (start us, length us, event | category | flops | bytes accessed | tf_op | source)
XLA Modules:
  0.0 160.7 jit_solution(5429769648572227848)
XLA Ops:
  0.6 158.6 %shard_map.85.both_ref = f32[88,128]{1,0:T(8,128)} custom-call(s32[1,64]{1,0:T(1,128)} %bitcast.10, bf16[80,128]{1,0:T(8,128)(2,1)} %bitcast.9, bf16[1188,640]{1,0:T(8,128)(2,1)} %bitcast.8, bf16[2,76032]{1,0:T(2,128)(2,1)} %tea_ref.1, s32[1,128]{1,0:T(1,128)} %bitcast.11, f32[1,128]{1,0:T(1,128)} %bitcast.12), custom_call_target="tpu_custom_call" | custom-call | tf_op jit(solution)/shard_map/pallas_call | solution.py:550
  159.2 1.4 shard_map.86

commit v4 on v3

--- a/solution.py
+++ b/solution.py
@@ -297,37 +297,42 @@
     m_s = jnp.full((1, TK), low, F32)
     m_t = jnp.full((1, TK), low, F32)
     for ch in range(NC):
+        t = tea(ch)
+        if ch == NC - 1:
+            t = jnp.where(lane < TAIL, t, low)
+        m_t = jnp.maximum(m_t, jnp.max(t, axis=0, keepdims=True))
+    s_tea = jnp.zeros((1, TK), F32)
+    for ch in range(NC):
+        et = jnp.exp(tea(ch) - m_t)
+        if ch == NC - 1:
+            et = jnp.where(lane < TAIL, et, 0.0)
+        s_tea = s_tea + jnp.sum(et, axis=0, keepdims=True)
+
+    for ch in range(NC):
         z_copy(ch).wait_recv()
         val = L[ch] + Rb[ch]
         L[ch] = val
-        t = tea(ch)
         if ch == NC - 1:
             val = jnp.where(lane < TAIL, val, low)
-            t = jnp.where(lane < TAIL, t, low)
         m_s = jnp.maximum(m_s, jnp.max(val, axis=0, keepdims=True))
-        m_t = jnp.maximum(m_t, jnp.max(t, axis=0, keepdims=True))
 
     s_sum = jnp.zeros((1, TK), F32)
     s_gap = jnp.zeros((1, TK), F32)
     s_pick = jnp.zeros((1, TK), F32)
-    s_tea = jnp.zeros((1, TK), F32)
     for ch in range(NC):
         val = L[ch]
         t = tea(ch)
         ex = jnp.exp(val - m_s)
-        et = jnp.exp(t - m_t)
         eg = ex * (val - t)
         pk = jnp.where(lane + ch * VC == here, val, 0.0)
         if ch == NC - 1:
             ok = lane < TAIL
             ex = jnp.where(ok, ex, 0.0)
-            et = jnp.where(ok, et, 0.0)
             eg = jnp.where(ok, eg, 0.0)
             pk = jnp.where(ok, pk, 0.0)
         s_sum = s_sum + jnp.sum(ex, axis=0, keepdims=True)
         s_gap = s_gap + jnp.sum(eg, axis=0, keepdims=True)
         s_pick = s_pick + jnp.sum(pk, axis=0, keepdims=True)
-        s_tea = s_tea + jnp.sum(et, axis=0, keepdims=True)
 
     row = lax.broadcasted_iota(jnp.int32, (8, TK), 0)
 

time: 161 us -> 161 us (level)
  no operation moved by 1% of the time
where the time goes in v4:
time: 161 us; the launch traced here: 160 us
  Pallas kernels  160 us (99%)
    pallas_call x1, Pallas kernels, on_device(): pl.pallas_call(kernel, out_shape=jax.ShapeDtypeStruct((OB + 8, TK), F32),...  158 us

profile of v4, /device:TPU:160, one launch (start us, length us, event | category | flops | bytes accessed | tf_op | source)
XLA Modules:
  0.0 160.3 jit_solution(12258555428646238519)
XLA Ops:
  0.6 158.2 %shard_map.85.both_ref = f32[88,128]{1,0:T(8,128)} custom-call(s32[1,64]{1,0:T(1,128)} %bitcast.10, bf16[80,128]{1,0:T(8,128)(2,1)} %bitcast.9, bf16[1188,640]{1,0:T(8,128)(2,1)} %bitcast.8, bf16[2,76032]{1,0:T(2,128)(2,1)} %tea_ref.1, s32[1,128]{1,0:T(1,128)} %bitcast.11, f32[1,128]{1,0:T(1,128)} %bitcast.12), custom_call_target="tpu_custom_call" | custom-call | tf_op jit(solution)/shard_map/pallas_call | solution.py:555
  158.9 1.4 shard_map.86
